TPU v7x, 32 devices: a whole 2x2x4 slice. The times are simulated.
32 devices in a mesh: wide: 8 (over z, y), seq: 4 (over x, core).
Axes of the slice: x: 2, y: 2, z: 4, core: 2. Of those that a mesh axis runs over, the one named last changes fastest.
Arguments:
- power: bfloat16 [160, 262144], P('seq', 'wide')
- bin_index: int32 [160], P('seq'), may hold values from 0 to 7, as said below
- session: int32 [2048], replicated, may hold values from 0 to 7, as said below
- readin_weight: bfloat16 [8, 128, 2048], P('wide'), may hold values from -0.5 to 0.5
- qkv_weight: bfloat16 [2048, 1536], replicated, may hold values from -0.125 to 0.125
Outputs:
- heads: bfloat16 [2048, 8, 1024], P(('wide', 'seq'))
Inputs may be any that keep to these rules, and one draw needn't show every extreme that they name: `bin_index`: the samples j * 40 to (j + 1) * 40 - 1 name only bins j * 2 to (j + 1) * 2 - 1. In each aligned block of 64 patches (patches k * 64 to (k + 1) * 64 - 1) no session is named by more than 16 patches; one session, the same for every block, is named by exactly 16 patches of every block.
All inputs are finite; a program needn't handle non-finite values.
Results may differ from a plain program's by a relative error of at most 0.008.
Values may be sent and summed in bfloat16 or wider, within the bound.
A program may use at most 64 MiB of HBM per device.

v0:
```python
import jax
import jax.numpy as jnp
from jax import lax
from jax.sharding import PartitionSpec as P

CH = 128
HD = 128
HEADS = 8
KVH = 2
SPB = 20


def attention_heads(qkv_rows):
    row_count = qkv_rows.shape[0]
    length = qkv_rows.shape[1]
    group_size = HEADS // KVH
    values = qkv_rows.astype(jnp.float32)
    queries = values[:, :, : HEADS * HD].reshape(row_count, length, KVH, group_size, HD)
    key_rows = values[:, :, HEADS * HD : (HEADS + KVH) * HD].reshape(row_count, length, KVH, HD)
    value_rows = values[:, :, (HEADS + KVH) * HD :].reshape(row_count, length, KVH, HD)
    queries = queries / jnp.sqrt(jnp.mean(queries * queries, axis=-1, keepdims=True) + 1e-06)
    key_rows = key_rows / jnp.sqrt(jnp.mean(key_rows * key_rows, axis=-1, keepdims=True) + 1e-06)
    scores = jnp.einsum("pigrd,pjgd->pgrij", queries, key_rows) / HD**0.5
    exponent = jnp.exp(scores)
    weights = (exponent / jnp.sum(exponent, axis=-1, keepdims=True)).astype(jnp.bfloat16)
    mixed = jnp.einsum("pgrij,pjgd->pigrd", weights.astype(jnp.float32), value_rows)
    return mixed.reshape(row_count, length, HEADS * HD).astype(jnp.bfloat16)


def project_rows(tokens, qkv_weight):
    product = jnp.dot(
        tokens.reshape(-1, tokens.shape[-1]), qkv_weight, preferred_element_type=jnp.float32
    )
    return product.astype(jnp.bfloat16).reshape(tokens.shape[:-1] + (qkv_weight.shape[1],))


def readin_rows(slab, weight_block):
    tokens = jnp.einsum(
        "abtc,cd->abtd", slab, weight_block, preferred_element_type=jnp.float32
    ).astype(jnp.bfloat16)
    return tokens


def slot_ranks(owner_ids, wide_count):
    owner_marks = (owner_ids[..., None] == jnp.arange(wide_count, dtype=jnp.int32)).astype(
        jnp.int32
    )
    running = jnp.cumsum(owner_marks, axis=-2)
    return jnp.sum(owner_marks * running, axis=-1) - 1


def body(power, bin_index, session, readin_weight, qkv_weight):
    wide_count = lax.axis_size("wide")
    seq_count = lax.axis_size("seq")
    wide_index = lax.axis_index("wide")
    seq_index = lax.axis_index("seq")
    sample_rows, channels = power.shape
    patch_count = channels // CH
    quarter = patch_count // seq_count
    bin_count = sample_rows // SPB
    capacity = max(2, 2 * quarter // wide_count)
    signal = power.astype(jnp.float32)
    squares = lax.psum(jnp.sum(signal * signal, axis=0), "seq")
    inv_rms = 1.0 / jnp.sqrt(squares / (sample_rows * seq_count) + 1e-06)
    active = jnp.maximum(signal * inv_rms[None, :] - 0.8, 0.0)
    local_bins = bin_index - seq_index * bin_count
    onehot = (local_bins[:, None] == jnp.arange(bin_count, dtype=jnp.int32)[None, :]).astype(
        jnp.float32
    )
    binned = (jnp.dot(onehot.T, active, precision=lax.Precision.HIGHEST) * (1.0 / SPB)).astype(
        jnp.bfloat16
    )
    patches = binned.reshape(bin_count, patch_count, CH).transpose(1, 0, 2)
    owners = lax.dynamic_slice_in_dim(session, wide_index * patch_count, patch_count)
    weight_block = readin_weight[0]
    owner_grid = owners.reshape(seq_count, quarter)
    slot_rank = slot_ranks(owner_grid, wide_count)
    quarter_ids = jnp.arange(seq_count, dtype=jnp.int32)[:, None]
    slot_index = ((owner_grid * seq_count + quarter_ids) * capacity + slot_rank).reshape(
        patch_count
    )
    slot_count = seq_count * capacity
    length = patches.shape[1]
    outgoing = (
        jnp.zeros((wide_count * slot_count, length, CH), jnp.bfloat16).at[slot_index].set(patches)
    )
    outgoing = outgoing.reshape(wide_count, slot_count, length, CH)
    returned_rows = lax.all_to_all(
        readin_rows(
            lax.all_to_all(outgoing, "wide", split_axis=0, concat_axis=0, tiled=True), weight_block
        ),
        "wide",
        split_axis=0,
        concat_axis=0,
        tiled=True,
    )
    arrived = returned_rows.reshape(
        wide_count * slot_count, returned_rows.shape[2], returned_rows.shape[3]
    )[slot_index]
    arrived = lax.all_to_all(arrived, "seq", split_axis=0, concat_axis=1, tiled=True)
    projected = project_rows(arrived, qkv_weight)
    return attention_heads(projected)


def solution(mesh):
    placed = (P("seq", "wide"), P("seq"), P(), P("wide", None, None), P())
    return jax.shard_map(
        body, mesh=mesh, in_specs=placed, out_specs=P(("wide", "seq"), None, None), check_vma=False
    )
```

profile of v0, /device:TPU:0, one launch (start us, length us, event | category | flops | bytes accessed | tf_op | source)
XLA Modules:
  0.0 255.3 jit_solution(1569734824458362901)
XLA Ops:
  6.5 3.3 %fusion.1 = f32[32768]{0:T(1024)} fusion(bf16[40,32768]{1,0:T(8,128)(2,1)} %param.5), kind=kLoop, calls=%fused_computation.6 | loop fusion | flops 3899392 | bytes 2752512 | tf_op jit(solution)/shard_map/reduce_sum | solution.py:63
  11.3 0.8 compare_select_fusion
  12.1 32.0 %all-reduce.2.cloned.1.call-done = f32[32768]{0:T(1024)} async-done(((f32[32768]{0:T(1024)}), f32[32768]{0:T(1024)}) %all-reduce.2.cloned.1.call-update) | async-done | bytes 131088 | tf_op jit(solution)/shard_map/psum | solution.py:63
  44.1 0.9 add_rsqrt_fusion
  45.0 2.5 fusion.11
  47.7 7.3 %scatter_fusion = bf16[512,2,128]{2,1,0:T(2,128)(2,1)S(1)} fusion(bf16[512,2,128]{2,1,0:T(2,128)(2,1)S(1)} %broadcast_in_dim.4, s32[256]{0:T(256)S(1)} %compare_select_fusion, bf16[256,2,128]{2,1,0:T(2,128)(2,1)S(1)} %fusion.11), kind=kCustom, calls=%fused_computation.1 | custom fusion | bytes 394240 | tf_op jit(solution)/shard_map/scatter | solution.py:85
  55.0 13.5 %all_to_all.25 = bf16[8,64,2,128]{3,1,2,0:T(8,128)(2,1)S(1)} all-to-all(bf16[8,64,2,128]{3,1,2,0:T(8,128)(2,1)S(1)} %copy.33), channel_id=1, replica_groups=mesh['wide'=8,'seq'=4] {'wide'}, dimensions={0} | all-to-all | bytes 524288 | tf_op jit(solution)/shard_map/all_to_all | solution.py:90
  68.5 3.2 %convolution_convert_fusion = bf16[8,64,2,2048]{3,1,2,0:T(8,128)(2,1)} fusion(bf16[8,64,2,128]{3,1,2,0:T(8,128)(2,1)S(1)} %all_to_all.25, bf16[1,128,2048]{2,1,0:T(8,128)(2,1)S(1)} %copy-done), kind=kOutput, calls=%fused_computation.9 | convolution fusion | flops 538968064 | bytes 4980736 | tf_op jit(solution)/shard_map/abtc,cd->abtd/dot_general | solution.py:38
  71.8 4.7 %all-to-all-start.1 = ((bf16[8,64,2,2048]{3,1,2,0:T(8,128)(2,1)}), bf16[8,64,2,2048]{3,1,2,0:T(8,128)(2,1)}, u32[]{:S(2)}, u32[]{:S(2)}) async-start(bf16[8,64,2,2048]{3,1,2,0:T(8,128)(2,1)} %convolution_convert_fusion), calls=%async_computation.1 | async-start | bytes 8388608 | tf_op jit(solution)/shard_map/all_to_all | solution.py:88
  76.5 90.8 %all-to-all-done.1 = bf16[8,64,2,2048]{3,1,2,0:T(8,128)(2,1)} async-done(((bf16[8,64,2,2048]{3,1,2,0:T(8,128)(2,1)}), bf16[8,64,2,2048]{3,1,2,0:T(8,128)(2,1)}, u32[]{:S(2)}, u32[]{:S(2)}) %all-to-all-start.1) | async-done | bytes 4194336 | tf_op jit(solution)/shard_map/all_to_all | solution.py:88
  167.3 2.5 copy.34
  169.8 6.2 %copy.35 = bf16[512,2,2048]{2,1,0:T(2,128)(2,1)} copy(bf16[512,2,2048]{2,0,1:T(8,128)(2,1)S(1)} %bitcast.52) | data formatting | bytes 8388608 | tf_op jit(solution)/shard_map/reshape | solution.py:97
  176.1 12.7 %gather_fusion = bf16[256,2,2048]{2,1,0:T(2,128)(2,1)S(1)} fusion(bf16[512,2,2048]{2,1,0:T(2,128)(2,1)} %copy.35, s32[1024]{0:T(1024)S(1)} %pad_clamp_fusion), kind=kCustom, calls=%fused_computation | custom fusion | bytes 4195328 | tf_op jit(solution)/shard_map/gather | solution.py:97
  188.8 28.2 %all_to_all.26 = bf16[256,2,2048]{2,1,0:T(2,128)(2,1)S(1)} all-to-all(bf16[256,2,2048]{2,1,0:T(2,128)(2,1)S(1)} %gather_fusion), channel_id=1, replica_groups=mesh['wide'=8,'seq'=4] {'seq'}, dimensions={0} | all-to-all | bytes 4194304 | tf_op jit(solution)/shard_map/all_to_all | solution.py:100
  217.0 2.5 copy.49
  219.5 2.2 reshape.56
  221.7 8.0 %fusion.24 = (f32[64,8,1536]{2,1,0:T(8,128)S(1)}, bf16[64,8,1536]{2,1,0:T(8,128)(2,1)}) fusion(bf16[512,2048]{1,0:T(8,128)(2,1)} %reshape.56, bf16[2048,1536]{1,0:T(8,128)(2,1)} %param.9), kind=kOutput, calls=%fused_computation.47 | convolution fusion | flops 3222798336 | bytes 13107200 | tf_op jit(solution)/shard_map/dot_general | solution.py:31
  229.8 1.7 copy-done.2
  231.9 1.5 slice.16
  233.4 0.8 multiply_reduce_fusion
  234.5 7.2 %fusion.9 = f32[64,2,8,8,4]{3,2,4,1,0:T(8,128)} fusion(f32[64,8,2,4,128]{4,1,3,2,0:T(8,128)S(1)} %bitcast.54, f32[64,8,2,4]{1,3,2,0:T(4,128)S(1)} %copy.40, f32[64,8,1536]{2,1,0:T(8,128)} %copy-done.2, f32[64,8,2]{1,2,0:T(2,128)S(1)} %copy.38), kind=kOutput, calls=%fused_computation.16 | convolution fusion | flops 9043968 | bytes 2772992 | tf_op jit(solution)/shard_map/pigrd,pjgd->pgrij/dot_general | solution.py:23
  241.7 2.7 %copy.41 = f32[64,2,8,8,4]{0,2,3,4,1:T(8,128)S(1)} copy(f32[64,2,8,8,4]{3,2,4,1,0:T(8,128)} %fusion.9) | data formatting | bytes 262144 | tf_op jit(solution)/shard_map/pigrd,pjgd->pgrij/dot_general | solution.py:23
  244.6 1.6 copy.42
  246.2 2.3 convolution_convert_fusion.2
  (31 shorter events, 2.7 us)
Async XLA Ops:
  6.5 62.0 %copy-start = (bf16[1,128,2048]{2,1,0:T(8,128)(2,1)S(1)}, bf16[1,128,2048]{2,1,0:T(8,128)(2,1)}, u32[]{:S(2)}) copy-start(bf16[1,128,2048]{2,1,0:T(8,128)(2,1)} %param.8) | copy-start | bytes 1572868
  6.5 38.5 %copy-start.1 = (bf16[40,32768]{1,0:T(8,128)(2,1)S(1)}, bf16[40,32768]{1,0:T(8,128)(2,1)}, u32[]{:S(2)}) copy-start(bf16[40,32768]{1,0:T(8,128)(2,1)} %param.5) | copy-start | bytes 7864324
  6.5 5.6 %copy-start.3 = (s32[40]{0:T(128)S(1)}, s32[40]{0:T(128)}, u32[]{:S(2)}) copy-start(s32[40]{0:T(128)} %param.6) | copy-start | bytes 484
  6.5 37.5 %all-reduce.2.cloned.1.call-start = ((), (), s32[]{:S(2)}) async-start(), calls=%async_computation.3 | async-start | bytes 262144 | tf_op jit(solution)/shard_map/psum | solution.py:63
  71.8 95.6 %all-to-all-start.1 = ((bf16[8,64,2,2048]{3,1,2,0:T(8,128)(2,1)}), bf16[8,64,2,2048]{3,1,2,0:T(8,128)(2,1)}, u32[]{:S(2)}, u32[]{:S(2)}) async-start(bf16[8,64,2,2048]{3,1,2,0:T(8,128)(2,1)} %convolution_convert_fusion), calls=%async_computation.1 | async-start | bytes 8388608 | tf_op jit(solution)/shard_map/all_to_all | solution.py:88
  229.8 1.7 copy-start.2
Sparse Core Ops, SparseCore 0:
  10.0 34.0 all-reduce.1
where the time goes:
time: 256 us; the launch traced here: 255 us
  waiting for transfers between devices  123 us (48%)
  local copies, waits for them, and re-layouts  42.5 us (17%)
  blocking collectives  41.7 us (16%)
  matrix products  23.3 us (9%)
  between operations  13.6 us (5%)
  other arithmetic  6.75 us (3%)
  starting transfers between devices  4.73 us (2%)
    all_to_all x1, waiting for transfers between devices, body(): lax.all_to_all(readin_rows(lax.all_to_all(outgoing, 'wide', split_axis=0,...  90.8 us
    psum x1, waiting for transfers between devices, body(): squares = lax.psum(jnp.sum(signal * signal, axis=0), 'seq')  32 us
    all_to_all x1, blocking collectives, body(): lax.all_to_all(arrived, 'seq', split_axis=0, concat_axis=1, tiled=True)  28.2 us
    all_to_all x1, blocking collectives, body(): lax.all_to_all(outgoing, 'wide', split_axis=0, concat_axis=0, tiled=True)  13.5 us
    gather x1, local copies, waits for them, and re-layouts, body(): returned_rows.reshape(wide_count * slot_count, returned_rows.shape[2], re...  12.7 us
    dot_general x1, matrix products, project_rows(): jnp.dot(tokens.reshape(-1, tokens.shape[-1]), qkv_weight, preferred_eleme...  8.04 us
    scatter x1, local copies, waits for them, and re-layouts, body(): jnp.zeros((wide_count * slot_count, length, CH), jnp.bfloat16)  7.27 us
    dot_general x1, matrix products, attention_heads(): scores = jnp.einsum('pigrd,pjgd->pgrij', queries, key_rows) / HD ** 0.5  7.2 us
  transfers between devices with their start and end apart: 2, of which 2 were waited for; matrix products, arithmetic and copies ran while one was open for 1% of the time, Pallas kernels for 0%

commit v1 on v0

v1 whole, which is shorter than its diff:
```python
import jax
import jax.numpy as jnp
from jax import lax
from jax.sharding import PartitionSpec as P

CH = 128
HD = 128
HEADS = 8
KVH = 2
SPB = 20


def attention_rows(qkv, length):
    rows = qkv.shape[0]
    block = 16 * length
    group = HEADS // KVH
    values = qkv.astype(jnp.float32).reshape(rows, HEADS + 2 * KVH, HD)
    scored = values[:, : HEADS + KVH]
    normed = scored / jnp.sqrt(jnp.mean(scored * scored, axis=-1, keepdims=True) + 1e-06)
    normed = normed.astype(jnp.bfloat16).reshape(rows // block, block, HEADS + KVH, HD)
    queries = normed[:, :, :HEADS].reshape(rows // block, block, KVH, group, HD)
    scores = jnp.einsum(
        "nigrd,njgd->ngrij", queries, normed[:, :, HEADS:], preferred_element_type=jnp.float32
    ) / HD**0.5
    at = jnp.arange(block, dtype=jnp.int32) // length
    exponent = jnp.where(at[:, None] == at[None, :], jnp.exp(scores), 0.0)
    weights = (exponent / jnp.sum(exponent, axis=-1, keepdims=True)).astype(jnp.bfloat16)
    value_rows = qkv[:, (HEADS + KVH) * HD :].reshape(rows // block, block, KVH, HD)
    mixed = jnp.einsum(
        "ngrij,njgd->nigrd", weights, value_rows, preferred_element_type=jnp.float32
    )
    return mixed.astype(jnp.bfloat16).reshape(rows // length, length, HEADS * HD)


def body(power, bin_index, session, readin_weight, qkv_weight):
    wide_count = lax.axis_size("wide")
    seq_count = lax.axis_size("seq")
    wide_index = lax.axis_index("wide")
    seq_index = lax.axis_index("seq")
    sample_rows, channels = power.shape
    patch_count = channels // CH
    quarter = patch_count // seq_count
    bin_count = sample_rows // SPB
    columns = qkv_weight.shape[1] // seq_count

    signal = power.astype(jnp.float32)
    squares = lax.psum(jnp.sum(signal * signal, axis=0), "seq")
    inv_rms = 1.0 / jnp.sqrt(squares / (sample_rows * seq_count) + 1e-06)
    active = jnp.maximum(signal * inv_rms[None, :] - 0.8, 0.0)
    local_bins = bin_index - seq_index * bin_count
    onehot = (local_bins[:, None] == jnp.arange(bin_count, dtype=jnp.int32)[None, :]).astype(
        jnp.float32
    )
    binned = (jnp.dot(onehot.T, active, precision=lax.Precision.HIGHEST) * (1.0 / SPB)).astype(
        jnp.bfloat16
    )
    binned = binned.reshape(bin_count, seq_count, quarter, CH).transpose(1, 2, 0, 3)
    patches = lax.all_to_all(binned, "seq", split_axis=0, concat_axis=0, tiled=True)
    length = seq_count * bin_count
    rows = patches.transpose(1, 0, 2, 3).reshape(quarter, length, CH)
    owners = lax.dynamic_slice_in_dim(
        session, (wide_index * seq_count + seq_index) * quarter, quarter
    )
    marks = owners[:, None] == jnp.arange(wide_count, dtype=jnp.int32)[None, :]
    spread = jnp.where(marks[:, None, :, None], rows[:, :, None, :], jnp.bfloat16(0))
    spread = spread.reshape(quarter * length, wide_count * CH)

    def project(block):
        folded = jnp.dot(readin_weight[0], block, preferred_element_type=jnp.float32)
        folded = lax.all_gather(folded.astype(jnp.bfloat16), "wide", axis=0, tiled=True)
        return jnp.dot(spread, folded, preferred_element_type=jnp.float32).astype(jnp.bfloat16)

    if wide_count > 8:
        blocks = qkv_weight.reshape(qkv_weight.shape[0], seq_count, -1).transpose(1, 0, 2)
        qkv = lax.map(project, blocks).transpose(1, 0, 2).reshape(quarter * length, -1)
    else:
        qkv = project(qkv_weight)
    return attention_rows(qkv, length)


def solution(mesh):
    placed = (P("seq", "wide"), P("seq"), P(), P("wide", None, None), P())
    return jax.shard_map(
        body, mesh=mesh, in_specs=placed, out_specs=P(("wide", "seq"), None, None), check_vma=False
    )
```

time: 256 us -> 99.2 us (0.39)
  waiting for transfers between devices: 123 us -> 54.4 us
  blocking collectives: 41.7 us -> 0 us
  local copies, waits for them, and re-layouts: 42.5 us -> 8.85 us
  matrix products: 23.3 us -> 12.1 us
    all_to_all x1, waiting for transfers between devices: 90.8 us -> 4.52 us  [body(): lax.all_to_all(binned, 'seq', split_axis=0, concat_axis=0, tiled=True)]
    all_to_all x2 -> x0, blocking collectives: 41.7 us -> none  [the longest x1 28.2 us: body(): lax.all_to_all(arrived, 'seq', split_axis=0, concat_axis=1, tiled=True)]
    all_gather x0 -> x1, waiting for transfers between devices: none -> 21.2 us  [project(): lax.all_gather(folded.astype(jnp.bfloat16), 'wide', axis=0, tiled=True)]
    gather x1 -> x0, local copies, waits for them, and re-layouts: 12.7 us -> none  [body(): returned_rows.reshape(wide_count * slot_count, returned_rows.shape[2], re...]
    dot_general x4, matrix products: 20.8 us -> 9.65 us  [the longest x1 4.68 us: project(): jnp.dot(readin_weight[0], block, preferred_element_type=jnp.float32)]
    scatter x1 -> x0, local copies, waits for them, and re-layouts: 7.27 us -> none  [body(): jnp.zeros((wide_count * slot_count, length, CH), jnp.bfloat16)]
    reshape x3, local copies, waits for them, and re-layouts: 8.53 us -> 2.98 us  [the longest x1 1.55 us: attention_rows(): mixed.astype(jnp.bfloat16).reshape(rows // length, length, HEADS * HD)]
    all_to_all x2 -> x0, local copies, waits for them, and re-layouts: 4.95 us -> none  [the longest x1 2.5 us: body(): lax.all_to_all(readin_rows(lax.all_to_all(outgoing, 'wide', split_axis=0,...]
  transfers between devices with their start and end apart: 2 -> 3, of which waited for: 2 -> 3; matrix products, arithmetic and copies ran while one was open for 1% -> 10% of each run, Pallas kernels for 0% -> 0%
where the time goes in v1:
time: 99.2 us; the launch traced here: 98.9 us
  waiting for transfers between devices  54.4 us (55%)
  between operations  15 us (15%)
  matrix products  12.1 us (12%)
  local copies, waits for them, and re-layouts  8.85 us (9%)
  other arithmetic  5.03 us (5%)
  starting transfers between devices  3.37 us (3%)
    psum x1, waiting for transfers between devices, body(): squares = lax.psum(jnp.sum(signal * signal, axis=0), 'seq')  28.7 us
    all_gather x1, waiting for transfers between devices, project(): lax.all_gather(folded.astype(jnp.bfloat16), 'wide', axis=0, tiled=True)  21.2 us
    dot_general x1, matrix products, project(): jnp.dot(readin_weight[0], block, preferred_element_type=jnp.float32)  4.68 us
    all_to_all x1, waiting for transfers between devices, body(): lax.all_to_all(binned, 'seq', split_axis=0, concat_axis=0, tiled=True)  4.52 us
    dot_general x1, matrix products, project(): jnp.dot(spread, folded, preferred_element_type=jnp.float32)  3.67 us
    all_to_all x1, starting transfers between devices, body(): lax.all_to_all(binned, 'seq', split_axis=0, concat_axis=0, tiled=True)  3.32 us
    reduce_sum x1, other arithmetic, body(): squares = lax.psum(jnp.sum(signal * signal, axis=0), 'seq')  3.17 us
    dot_general x1, matrix products, body(): jnp.dot(onehot.T, active, precision=lax.Precision.HIGHEST) * (1.0 / SPB)  2.49 us
  transfers between devices with their start and end apart: 3, of which 3 were waited for; matrix products, arithmetic and copies ran while one was open for 10% of the time, Pallas kernels for 0%

profile of v1, /device:TPU:0, one launch (start us, length us, event | category | flops | bytes accessed | tf_op | source)
XLA Modules:
  0.0 98.9 jit_solution(4633290548745666864)
XLA Ops:
  7.4 3.2 %fusion.1 = f32[32768]{0:T(1024)} fusion(bf16[40,32768]{1,0:T(8,128)(2,1)} %param.5), kind=kLoop, calls=%fused_computation.4 | loop fusion | flops 3899392 | bytes 2752512 | tf_op jit(solution)/shard_map/reduce_sum | solution.py:47
  10.6 4.7 %convolution_convert_fusion.1 = bf16[128,1536]{1,0:T(8,128)(2,1)} fusion(bf16[2048,1536]{1,0:T(8,128)(2,1)} %param.9, bf16[1,128,2048]{2,1,0:T(8,128)(2,1)S(1)} %copy-done), kind=kOutput, calls=%fused_computation.15 | convolution fusion | flops 805502976 | bytes 7208960 | tf_op jit(solution)/shard_map/dot_general | solution.py:69
  15.4 0.8 dynamic_slice.3
  16.2 28.7 %all-reduce.2.cloned.1.call-done = f32[32768]{0:T(1024)} async-done(((f32[32768]{0:T(1024)}), f32[32768]{0:T(1024)}) %all-reduce.2.cloned.1.call-update) | async-done | bytes 131088 | tf_op jit(solution)/shard_map/psum | solution.py:47
  44.9 0.9 add_rsqrt_fusion
  45.9 2.5 %fusion.12 = bf16[1,2,256,128]{3,1,2,0:T(2,128)(2,1)S(1)} fusion(bf16[40,32768]{1,0:T(8,128)(2,1)S(1)} %copy-done.1, f32[32768]{0:T(1024)S(1)} %add_rsqrt_fusion, s32[40]{0:T(128)S(1)} %broadcast_subtract_fusion), kind=kOutput, calls=%fused_computation.21 | convolution fusion | flops 36831312 | bytes 2883744 | tf_op jit(solution)/shard_map/dot_general | solution.py:54
  48.4 0.7 copy.36
  49.1 3.3 %all-to-all-start = ((bf16[4,64,2,128]{3,1,2,0:T(8,128)(2,1)}), bf16[4,64,2,128]{3,1,2,0:T(8,128)(2,1)S(1)}, u32[]{:S(2)}, u32[]{:S(2)}) async-start(bf16[4,64,2,128]{3,1,2,0:T(8,128)(2,1)} %bitcast.41), calls=%async_computation | async-start | bytes 262144 | tf_op jit(solution)/shard_map/all_to_all | solution.py:58
  52.5 4.5 %all-to-all-done = bf16[4,64,2,128]{3,1,2,0:T(8,128)(2,1)S(1)} async-done(((bf16[4,64,2,128]{3,1,2,0:T(8,128)(2,1)}), bf16[4,64,2,128]{3,1,2,0:T(8,128)(2,1)S(1)}, u32[]{:S(2)}, u32[]{:S(2)}) %all-to-all-start) | async-done | bytes 131104 | tf_op jit(solution)/shard_map/all_to_all | solution.py:58
  57.1 0.2 select_bitcast_fusion
  57.3 21.2 %all-gather.2.cloned.1.call-done = bf16[1024,1536]{1,0:T(8,128)(2,1)} async-done(((bf16[128,1536]{1,0:T(8,128)(2,1)}), bf16[1024,1536]{1,0:T(8,128)(2,1)}) %all-gather.2.cloned.1.call-update) | async-done | bytes 3145744 | tf_op jit(solution)/shard_map/all_gather | solution.py:70
  78.4 3.7 %convolution_convert_fusion = bf16[512,1536]{1,0:T(8,128)(2,1)S(1)} fusion(bf16[1024,1536]{1,0:T(8,128)(2,1)} %all-gather.2.cloned.1.call-done, bf16[64,8,8,128]{3,2,1,0:T(8,128)(2,1)S(1)} %select_bitcast_fusion), kind=kOutput, calls=%fused_computation.9 | convolution fusion | flops 1611399168 | bytes 5767168 | tf_op jit(solution)/shard_map/dot_general | solution.py:71
  82.1 1.2 %copy-done.2 = bf16[512,1536]{1,0:T(8,128)(2,1)} copy-done((bf16[512,1536]{1,0:T(8,128)(2,1)}, bf16[512,1536]{1,0:T(8,128)(2,1)S(1)}, u32[]{:S(2)}) %copy-start.2) | copy-done | bytes 1572888
  83.3 1.8 %copy.10 = bf16[512,1536]{0,1:T(8,128)(2,1)S(1)} copy(bf16[512,1536]{1,0:T(8,128)(2,1)} %copy-done.2) | data formatting | bytes 3145728 | tf_op jit(solution)/shard_map/convert_element_type | solution.py:71
  85.1 0.8 reshape.83
  85.8 0.3 fusion.5
  86.2 0.3 fusion.6
  86.4 0.8 copy.11
  87.3 0.1 copy.13
  87.5 0.6 fusion.10
  88.1 0.4 copy-done.3
  88.4 0.7 fusion.11
  89.1 0.7 copy.16
  89.9 1.5 %reshape.87 = bf16[64,8,1024]{2,1,0:T(8,128)(2,1)} reshape(bf16[4,128,2,4,128]{4,3,2,1,0:T(4,128)(2,1)S(1)} %copy.16) | data formatting | bytes 2097152 | tf_op jit(solution)/shard_map/reshape | solution.py:32
  (22 shorter events, 0.5 us)
Async XLA Ops:
  7.4 3.3 %copy-start = (bf16[1,128,2048]{2,1,0:T(8,128)(2,1)S(1)}, bf16[1,128,2048]{2,1,0:T(8,128)(2,1)}, u32[]{:S(2)}) copy-start(bf16[1,128,2048]{2,1,0:T(8,128)(2,1)} %param.8) | copy-start | bytes 1572868
  7.4 37.6 %all-reduce.2.cloned.1.call-start = ((), (), s32[]{:S(2)}) async-start(), calls=%async_computation.1 | async-start | bytes 262144 | tf_op jit(solution)/shard_map/psum | solution.py:47
  10.6 5.6 %copy-start.4 = (s32[40]{0:T(128)S(1)}, s32[40]{0:T(128)}, u32[]{:S(2)}) copy-start(s32[40]{0:T(128)} %param.6) | copy-start | bytes 484
  10.6 35.3 %copy-start.1 = (bf16[40,32768]{1,0:T(8,128)(2,1)S(1)}, bf16[40,32768]{1,0:T(8,128)(2,1)}, u32[]{:S(2)}) copy-start(bf16[40,32768]{1,0:T(8,128)(2,1)} %param.5) | copy-start | bytes 7864324
  10.6 67.9 %all-gather.2.cloned.1.call-start = ((), (), s32[]{:S(2)}) async-start(), calls=%async_computation.2 | async-start | bytes 3538944 | tf_op jit(solution)/shard_map/all_gather | solution.py:70
  49.1 7.9 %all-to-all-start = ((bf16[4,64,2,128]{3,1,2,0:T(8,128)(2,1)}), bf16[4,64,2,128]{3,1,2,0:T(8,128)(2,1)S(1)}, u32[]{:S(2)}, u32[]{:S(2)}) async-start(bf16[4,64,2,128]{3,1,2,0:T(8,128)(2,1)} %bitcast.41), calls=%async_computation | async-start | bytes 262144 | tf_op jit(solution)/shard_map/all_to_all | solution.py:58
  82.1 1.2 %copy-start.2 = (bf16[512,1536]{1,0:T(8,128)(2,1)}, bf16[512,1536]{1,0:T(8,128)(2,1)S(1)}, u32[]{:S(2)}) copy-start(bf16[512,1536]{1,0:T(8,128)(2,1)S(1)} %convolution_convert_fusion) | copy-start | bytes 4718596
  83.3 1.8 %slice-start = ((bf16[512,1536]{1,0:T(8,128)(2,1)}), bf16[512,256]{1,0:T(8,128)(2,1)S(1)}, s32[]{:S(2)}) async-start(bf16[512,1536]{1,0:T(8,128)(2,1)} %copy-done.2), calls=%async_computation.3 | async-start | bytes 524288 | tf_op jit(solution)/shard_map/slice | solution.py:28
  87.5 1.0 copy-start.3
Sparse Core Ops, SparseCore 0:
  10.7 34.2 all-reduce.1
Sparse Core Ops, SparseCore 1:
  15.4 63.0 all-gather.1

commit v2 on v1

--- a/solution.py
+++ b/solution.py
@@ -1,6 +1,8 @@
 import jax
 import jax.numpy as jnp
 from jax import lax
+from jax.experimental import pallas as pl
+from jax.experimental.pallas import tpu as pltpu
 from jax.sharding import PartitionSpec as P
 
 CH = 128
@@ -78,8 +80,375 @@
     return attention_rows(qkv, length)
 
 
+def kernel(
+    power_hbm, bin_ref, session_ref, readin_hbm, weight_hbm, out_ref,
+    power_v, readin_v, weight_v, folded, mask, spread, qkv,
+    sq_own, sq_in, inv, bin_out, bin_in,
+    load_sem, fold_send, fold_recv, seq_send, seq_recv,
+):
+    wide, seq = lax.axis_index("wide"), lax.axis_index("seq")
+    seq_count, quarter, _ = sq_own.shape
+    samples, channels = power_v.shape
+    sessions = folded.shape[1]
+    columns = folded.shape[3]
+    bins = bin_out.shape[1] // quarter
+    length = bins * seq_count
+    z, y = lax.div(wide, 2), lax.rem(wide, 2)
+    x, core = lax.div(seq, 2), lax.rem(seq, 2)
+    flip_y, flip_x = 1 - 2 * y, 2 - 4 * x
+
+    def paired(index, t):
+        return (index, index + 1 - 2 * lax.rem(index, 2), lax.rem(index + 2, 4), 3 - index)[t]
+
+    loads = [
+        pltpu.make_async_copy(readin_hbm.at[0], readin_v, load_sem.at[4]),
+        pltpu.make_async_copy(
+            weight_hbm.at[:, pl.ds(pl.multiple_of(seq * columns, 128), columns)],
+            weight_v,
+            load_sem.at[5],
+        ),
+    ]
+    for load in loads:
+        load.start()
+    part = channels // seq_count
+
+    def power_load(q):
+        at = pl.ds(pl.multiple_of(q * part, 128), part)
+        return pltpu.make_async_copy(power_hbm.at[:, at], power_v.at[:, at], load_sem.at[q])
+
+    for q in range(seq_count):
+        power_load(q).start()
+
+    barrier = pltpu.get_barrier_semaphore()
+
+    def greet(device):
+        pl.semaphore_signal(
+            barrier, inc=1, device_id=device, device_id_type=pl.DeviceIdType.MESH
+        )
+
+    for d in range(1, 4):
+        greet((wide, paired(seq, d)))
+    greet((wide + flip_y, seq))
+
+    @pl.when(z > 0)
+    def _():
+        greet((wide - 2, seq))
+
+    @pl.when(z < 3)
+    def _():
+        greet((wide + 2, seq))
+
+    for load in loads:
+        load.wait()
+    folded[seq, wide] = jnp.dot(
+        readin_v[...], weight_v[...], preferred_element_type=jnp.float32
+    ).astype(jnp.bfloat16)
+
+    peers = 4 + jnp.where(z > 0, 1, 0) + jnp.where(z < 3, 1, 0)
+    pl.semaphore_wait(barrier, peers)
+
+    first = (wide + (1 - core) * flip_y, seq + core * flip_x)
+    second = (wide + core * flip_y, seq + (1 - core) * flip_x)
+    other_core = (wide, seq + 1 - 2 * core)
+    lines = (
+        (seq, y),
+        (first[1], lax.rem(first[0], 2)),
+        (second[1], lax.rem(second[0], 2)),
+        (seq + flip_x, 1 - y),
+    )
+
+    def piece(line, t):
+        return lines[line][0], paired(z, t) * 2 + lines[line][1]
+
+    def fold_copy(at, sem, device):
+        return pltpu.make_async_remote_copy(
+            src_ref=folded.at[at[0], at[1]],
+            dst_ref=folded.at[at[0], at[1]],
+            send_sem=fold_send.at[sem],
+            recv_sem=fold_recv.at[at[0], at[1]],
+            device_id=device,
+            device_id_type=pl.DeviceIdType.MESH,
+        )
+
+    def along_z(t, act):
+        at = piece(0, t)
+        here = paired(z, t)
+
+        @pl.when(jnp.logical_and(here <= z, z < 3))
+        def _():
+            act(fold_copy(at, t, (wide + 2, seq)))
+
+        @pl.when(jnp.logical_and(here >= z, z > 0))
+        def _():
+            act(fold_copy(at, 4 + t, (wide - 2, seq)))
+
+    def onward(line, t, act):
+        at = piece(line, t)
+        if line == 0:
+            act(fold_copy(at, 8 + t, first))
+        if line < 2:
+            act(fold_copy(at, 12 + 4 * line + t, second))
+        act(fold_copy(at, 20 + 4 * line + t, other_core))
+
+    def start(copy):
+        copy.start()
+
+    def wait_send(copy):
+        copy.wait_send()
+
+    def relay(line, t):
+        if line or t:
+            fold_copy(piece(line, t), 0, other_core).wait_recv()
+        if line == 0:
+            along_z(t, start)
+        onward(line, t, start)
+
+    relay(0, 0)
+
+    def seq_copy(kind, source, target, d):
+        return pltpu.make_async_remote_copy(
+            src_ref=source,
+            dst_ref=target,
+            send_sem=seq_send.at[kind, d],
+            recv_sem=seq_recv.at[kind, d],
+            device_id=(wide, paired(seq, d)),
+            device_id_type=pl.DeviceIdType.MESH,
+        )
+
+    def patch_rows(q, c):
+        at = pl.multiple_of(q * part + c * 16 * CH, 16 * CH)
+        return power_v[:, pl.ds(at, 16 * CH)].astype(jnp.float32)
+
+    def square_copy(d):
+        return seq_copy(0, sq_own.at[paired(seq, d)], sq_in.at[d], d)
+
+    for d in (2, 3, 1, 0):
+        q = paired(seq, d)
+        power_load(q).wait()
+
+        @pl.loop(0, quarter // 16)
+        def _(c):
+            signal = patch_rows(q, c)
+            signal = signal * signal
+            sums = [
+                jnp.sum(signal[:, k * CH : (k + 1) * CH], axis=0, keepdims=True) for k in range(16)
+            ]
+            sq_own[q, pl.ds(pl.multiple_of(c * 16, 16), 16), :] = jnp.concatenate(sums, axis=0)
+
+        if d:
+            square_copy(d).start()
+
+    rows = quarter * length
+    device = wide * seq_count + seq
+    session_row = session_ref[pl.ds(lax.div(device * quarter, 128), 1), :]
+    named = (
+        session_row == lax.broadcasted_iota(jnp.int32, (sessions, 128), 0)
+    ).astype(jnp.bfloat16)
+    lane = lax.broadcasted_iota(jnp.int32, (rows, 128), 1)
+    row = lax.broadcasted_iota(jnp.int32, (rows, 128), 0)
+    own = (
+        lane == lax.rem(device * quarter, 128) + lax.div(row, length)
+    ).astype(jnp.bfloat16)
+    chosen = lax.dot_general(
+        own, named, (((1,), (1,)), ((), ())), preferred_element_type=jnp.float32
+    ).astype(jnp.bfloat16)
+    widen = (
+        lax.broadcasted_iota(jnp.int32, (sessions, sessions * CH), 0)
+        == lax.div(lax.broadcasted_iota(jnp.int32, (sessions, sessions * CH), 1), CH)
+    ).astype(jnp.bfloat16)
+    mask[...] = jnp.dot(chosen, widen, preferred_element_type=jnp.float32).astype(jnp.bfloat16)
+
+    diagonal = lax.broadcasted_iota(jnp.int32, (samples, samples), 0) == lax.broadcasted_iota(
+        jnp.int32, (samples, samples), 1
+    )
+    local_bin = jnp.sum(
+        jnp.where(diagonal, (bin_ref[...] - seq * bins).astype(jnp.float32), 0.0),
+        axis=1,
+        keepdims=True,
+    )
+    in_bin = [
+        jnp.broadcast_to((local_bin == b).astype(jnp.float32), (samples, CH)) for b in range(bins)
+    ]
+
+    relay(0, 1)
+
+    total = sq_own[seq]
+    for d in range(1, 4):
+        square_copy(d).wait_recv()
+        total = total + sq_in[d]
+    inv[0] = 1.0 / jnp.sqrt(total / (samples * seq_count) + 1e-06)
+
+    def inv_copy(d):
+        return seq_copy(1, inv.at[0], inv.at[d], d)
+
+    for d in (2, 3, 1):
+        inv_copy(d).start()
+
+    def bin_quarter(d, target):
+        q = paired(seq, d)
+
+        @pl.loop(0, quarter // 16)
+        def _(c):
+            signal = patch_rows(q, c)
+            at = pl.multiple_of(c * 16, 16)
+            scale = inv[d, pl.ds(at, 16), :]
+            found = [[] for _ in range(bins)]
+            for k in range(16):
+                active = jnp.maximum(
+                    signal[:, k * CH : (k + 1) * CH] * scale[k : k + 1] - 0.8, 0.0
+                )
+                for b in range(bins):
+                    found[b].append(jnp.sum(active * in_bin[b], axis=0, keepdims=True))
+            for b in range(bins):
+                target[d, pl.ds(pl.multiple_of(b * quarter + c * 16, 16), 16), :] = (
+                    jnp.concatenate(found[b], axis=0) * (1.0 / SPB)
+                ).astype(jnp.bfloat16)
+
+    def bin_copy(d):
+        return seq_copy(2, bin_out.at[d], bin_in.at[d], d)
+
+    bin_quarter(0, bin_in)
+    relay(0, 2)
+    for d in (2, 3, 1):
+        inv_copy(d).wait_recv()
+        bin_quarter(d, bin_out)
+        bin_copy(d).start()
+        if d == 2:
+            relay(0, 3)
+            relay(1, 0)
+        if d == 3:
+            relay(1, 1)
+    relay(1, 2)
+    relay(1, 3)
+    for t in range(4):
+        relay(2, t)
+    for t in range(4):
+        relay(3, t)
+
+    block = 16 * length
+    r = lax.broadcasted_iota(jnp.int32, (block, block), 0)
+    c = lax.broadcasted_iota(jnp.int32, (block, block), 1)
+    turn = jnp.logical_and(
+        lax.div(r, length) == lax.rem(c, 16), lax.rem(r, length) == lax.div(c, 16)
+    ).astype(jnp.bfloat16)
+    for d in range(1, 4):
+        bin_copy(d).wait_recv()
+    for n in range(quarter // 16):
+        pieces = []
+        for owner in range(seq_count):
+            slot = owner + seq - 2 * (
+                lax.rem(owner, 2) * lax.rem(seq, 2) + 2 * (owner // 2) * lax.div(seq, 2)
+            )
+            for b in range(bins):
+                pieces.append(bin_in[slot, b * quarter + n * 16 : b * quarter + n * 16 + 16, :])
+        turned = jnp.dot(
+            turn, jnp.concatenate(pieces, axis=0), preferred_element_type=jnp.float32
+        ).astype(jnp.bfloat16)
+        at = slice(n * block, (n + 1) * block)
+        spread[at, :] = mask[at, :] * jnp.concatenate([turned] * sessions, axis=1)
+
+    for line in range(4):
+        for t in range(4):
+            at = piece(line, t)
+            fold_copy((at[0] + 1 - 2 * core, at[1]), 0, other_core).wait_recv()
+
+    for n in range(seq_count):
+        weights = folded[n].reshape(sessions * CH, columns)
+        qkv[:, n * columns : (n + 1) * columns] = jnp.dot(
+            spread[...], weights, preferred_element_type=jnp.float32
+        ).astype(jnp.bfloat16)
+
+    group = HEADS // KVH
+    same = lax.div(lax.broadcasted_iota(jnp.int32, (group * block, block), 0), length)
+    same = lax.rem(same, 16) == lax.div(
+        lax.broadcasted_iota(jnp.int32, (group * block, block), 1), length
+    )
+
+    @pl.loop(0, quarter // 16)
+    def _(n):
+        at = pl.ds(pl.multiple_of(n * block, block), block)
+
+        def normed(h, scale):
+            values = qkv[at, h * HD : (h + 1) * HD].astype(jnp.float32)
+            mean = jnp.mean(values * values, axis=-1, keepdims=True)
+            return (values * (lax.rsqrt(mean + 1e-06) * scale)).astype(jnp.bfloat16)
+
+        for g in range(KVH):
+            keys = normed(HEADS + g, 1.0)
+            heads = range(g * group, (g + 1) * group)
+            queries = jnp.concatenate([normed(h, HD**-0.5) for h in heads], axis=0)
+            scores = lax.dot_general(
+                queries, keys, (((1,), (1,)), ((), ())), preferred_element_type=jnp.float32
+            )
+            exponent = jnp.where(same, jnp.exp(scores), 0.0)
+            weights = exponent * (1.0 / jnp.sum(exponent, axis=-1, keepdims=True))
+            mixed = jnp.dot(
+                weights.astype(jnp.bfloat16),
+                qkv[at, (HEADS + KVH + g) * HD : (HEADS + KVH + g + 1) * HD],
+                preferred_element_type=jnp.float32,
+            )
+            for i, h in enumerate(heads):
+                own_rows = mixed[i * block : (i + 1) * block].reshape(16, length, HD)
+                out_ref[pl.ds(n * 16, 16), :, h * HD : (h + 1) * HD] = own_rows.astype(
+                    jnp.bfloat16
+                )
+
+    for d in range(1, 4):
+        square_copy(d).wait_send()
+        inv_copy(d).wait_send()
+        bin_copy(d).wait_send()
+    for line in range(4):
+        for t in range(4):
+            if line == 0:
+                along_z(t, wait_send)
+            onward(line, t, wait_send)
+
+
+def fused(power, bin_index, session, readin_weight, qkv_weight):
+    samples, channels = power.shape
+    seq_count, sessions = lax.axis_size("seq"), lax.axis_size("wide")
+    quarter = channels // CH // seq_count
+    bins = samples // SPB
+    columns = qkv_weight.shape[1] // seq_count
+    rows = quarter * bins * seq_count
+    width = readin_weight.shape[2]
+    hbm = pl.BlockSpec(memory_space=pl.ANY)
+    vmem = pl.BlockSpec(memory_space=pltpu.VMEM)
+    bf16, f32 = jnp.bfloat16, jnp.float32
+    dma = pltpu.SemaphoreType.DMA
+    return pl.pallas_call(
+        kernel,
+        out_shape=jax.ShapeDtypeStruct((quarter, bins * seq_count, HEADS * HD), bf16),
+        in_specs=[hbm, vmem, vmem, hbm, hbm],
+        out_specs=vmem,
+        scratch_shapes=[
+            pltpu.VMEM((samples, channels), bf16),
+            pltpu.VMEM((CH, width), bf16),
+            pltpu.VMEM((width, columns), bf16),
+            pltpu.VMEM((seq_count, sessions, CH, columns), bf16),
+            pltpu.VMEM((rows, sessions * CH), bf16),
+            pltpu.VMEM((rows, sessions * CH), bf16),
+            pltpu.VMEM((rows, qkv_weight.shape[1]), bf16),
+            pltpu.VMEM((seq_count, quarter, CH), f32),
+            pltpu.VMEM((seq_count, quarter, CH), f32),
+            pltpu.VMEM((seq_count, quarter, CH), f32),
+            pltpu.VMEM((seq_count, bins * quarter, CH), bf16),
+            pltpu.VMEM((seq_count, bins * quarter, CH), bf16),
+            dma((6,)),
+            dma((36,)),
+            dma((seq_count, sessions)),
+            dma((3, seq_count)),
+            dma((3, seq_count)),
+        ],
+        compiler_params=pltpu.CompilerParams(
+            collective_id=0, has_side_effects=True, vmem_limit_bytes=40 * 2**20
+        ),
+    )(power, bin_index.reshape(1, samples), session.reshape(-1, 128), readin_weight, qkv_weight)
+
+
 def solution(mesh):
+    fits = dict(mesh.shape) == {"wide": 8, "seq": 4}
     placed = (P("seq", "wide"), P("seq"), P(), P("wide", None, None), P())
     return jax.shard_map(
-        body, mesh=mesh, in_specs=placed, out_specs=P(("wide", "seq"), None, None), check_vma=False
-    )
+        fused if fits else body, mesh=mesh, in_specs=placed, out_specs=P(("wide", "seq"), None, None), check_vma=False
+    )

time: 99.2 us -> 44.3 us (0.45)
  waiting for transfers between devices: 54.4 us -> 0 us
  Pallas kernels: 0 us -> 35.5 us
  between operations: 15 us -> 0.01 us
  matrix products: 12.1 us -> 0 us
  other arithmetic: 5.03 us -> 0 us
  starting transfers between devices: 3.37 us -> 0 us
    pallas_call x0 -> x1, Pallas kernels: none -> 35.5 us  [fused(): pl.pallas_call(kernel, out_shape=jax.ShapeDtypeStruct((quarter, bins * se...]
    psum x1 -> x0, waiting for transfers between devices: 28.7 us -> none  [body(): squares = lax.psum(jnp.sum(signal * signal, axis=0), 'seq')]
    all_gather x1 -> x0, waiting for transfers between devices: 21.2 us -> none  [project(): lax.all_gather(folded.astype(jnp.bfloat16), 'wide', axis=0, tiled=True)]
    dot_general x5 -> x0, matrix products: 12.1 us -> none  [the longest x1 4.68 us: project(): jnp.dot(readin_weight[0], block, preferred_element_type=jnp.float32)]
    unnamed x11, local copies, waits for them, and re-layouts: 1.56 us -> 7.89 us
    all_to_all x1 -> x0, waiting for transfers between devices: 4.52 us -> none  [body(): lax.all_to_all(binned, 'seq', split_axis=0, concat_axis=0, tiled=True)]
    reduce_sum x2 -> x0, other arithmetic: 3.46 us -> none  [the longest x1 3.17 us: body(): squares = lax.psum(jnp.sum(signal * signal, axis=0), 'seq')]
    all_to_all x1 -> x0, starting transfers between devices: 3.32 us -> none  [body(): lax.all_to_all(binned, 'seq', split_axis=0, concat_axis=0, tiled=True)]
  transfers between devices with their start and end apart: 3 -> 0, of which waited for: 3 -> 0; matrix products, arithmetic and copies ran while one was open for 10% -> 0% of each run, Pallas kernels for 0% -> 0%
where the time goes in v2:
time: 44.3 us; the launch traced here: 43.4 us
  Pallas kernels  35.5 us (80%)
  local copies, waits for them, and re-layouts  7.89 us (18%)
    pallas_call x1, Pallas kernels, fused(): pl.pallas_call(kernel, out_shape=jax.ShapeDtypeStruct((quarter, bins * se...  35.5 us
    unnamed x11, local copies, waits for them, and re-layouts  7.89 us

profile of v2, /device:TPU:0, one launch (start us, length us, event | category | flops | bytes accessed | tf_op | source)
XLA Modules:
  0.0 43.4 jit_solution(18229750540757447690)
XLA Ops:
  0.0 0.0 copy-start
  0.0 2.8 %copy-done = bf16[2048,1536]{1,0:T(8,128)(2,1)S(1)} copy-done((bf16[2048,1536]{1,0:T(8,128)(2,1)S(1)}, bf16[2048,1536]{1,0:T(8,128)(2,1)}, u32[]{:S(2)}) %copy-start) | copy-done | bytes 6291480
  2.8 0.0 copy-start.1
  2.8 1.7 %copy-done.1 = bf16[40,32768]{1,0:T(8,128)(2,1)S(1)} copy-done((bf16[40,32768]{1,0:T(8,128)(2,1)S(1)}, bf16[40,32768]{1,0:T(8,128)(2,1)}, u32[]{:S(2)}) %copy-start.1) | copy-done | bytes 2621464
  4.5 0.0 copy-start.2
  4.5 1.0 %copy-done.2 = bf16[1,128,2048]{2,1,0:T(8,128)(2,1)S(1)} copy-done((bf16[1,128,2048]{2,1,0:T(8,128)(2,1)S(1)}, bf16[1,128,2048]{2,1,0:T(8,128)(2,1)}, u32[]{:S(2)}) %copy-start.2) | copy-done | bytes 524312
  5.6 0.0 copy-start.3
  5.6 0.7 %copy-done.3 = s32[2048]{0:T(1024)S(1)} copy-done((s32[2048]{0:T(1024)S(1)}, s32[2048]{0:T(1024)}, u32[]{:S(2)}) %copy-start.3) | copy-done | bytes 8216
  6.3 0.0 copy-start.4
  6.3 0.7 %copy-done.4 = s32[40]{0:T(128)S(1)} copy-done((s32[40]{0:T(128)S(1)}, s32[40]{0:T(128)}, u32[]{:S(2)}) %copy-start.4) | copy-done | bytes 184
  6.9 35.5 %shard_map.55 = bf16[64,8,1024]{2,1,0:T(8,128)(2,1)S(1)} custom-call(bf16[40,32768]{1,0:T(8,128)(2,1)S(1)} %copy-done.1, s32[1,40]{1,0:T(1,128)S(1)} %bitcast.3, s32[16,128]{1,0:T(8,128)S(1)} %bitcast.2, bf16[1,128,2048]{2,1,0:T(8,128)(2,1)S(1)} %copy-done.2, bf16[2048,1536]{1,0:T(8,128)(2,1)S(1)} %copy-done), custom_call_target="tpu_custom_call" | custom-call | tf_op jit(solution)/shard_map/pallas_call | solution.py:419
  42.5 1.0 %copy.7 = bf16[64,8,1024]{2,1,0:T(8,128)(2,1)} copy(bf16[64,8,1024]{2,1,0:T(8,128)(2,1)S(1)} %shard_map.55) | data formatting | bytes 2097152
Async XLA Ops:
  0.0 2.8 %copy-start = (bf16[2048,1536]{1,0:T(8,128)(2,1)S(1)}, bf16[2048,1536]{1,0:T(8,128)(2,1)}, u32[]{:S(2)}) copy-start(bf16[2048,1536]{1,0:T(8,128)(2,1)} %weight_hbm.1) | copy-start | bytes 18874372
  2.8 1.7 %copy-start.1 = (bf16[40,32768]{1,0:T(8,128)(2,1)S(1)}, bf16[40,32768]{1,0:T(8,128)(2,1)}, u32[]{:S(2)}) copy-start(bf16[40,32768]{1,0:T(8,128)(2,1)} %power_hbm.1) | copy-start | bytes 7864324
  4.5 1.0 %copy-start.2 = (bf16[1,128,2048]{2,1,0:T(8,128)(2,1)S(1)}, bf16[1,128,2048]{2,1,0:T(8,128)(2,1)}, u32[]{:S(2)}) copy-start(bf16[1,128,2048]{2,1,0:T(8,128)(2,1)} %readin_hbm.1) | copy-start | bytes 1572868
  5.6 0.7 %copy-start.3 = (s32[2048]{0:T(1024)S(1)}, s32[2048]{0:T(1024)}, u32[]{:S(2)}) copy-start(s32[2048]{0:T(1024)} %param.7) | copy-start | bytes 24580
  6.3 0.7 %copy-start.4 = (s32[40]{0:T(128)S(1)}, s32[40]{0:T(128)}, u32[]{:S(2)}) copy-start(s32[40]{0:T(128)} %param.6) | copy-start | bytes 484

commit v3 on v2

--- a/solution.py
+++ b/solution.py
@@ -81,7 +81,8 @@
 
 
 def kernel(
-    power_hbm, bin_ref, session_ref, readin_hbm, weight_hbm, out_ref,
+    power_hbm, bin_hbm, session_hbm, readin_hbm, weight_hbm, out_ref,
+    bin_ref, session_ref,
     power_v, readin_v, weight_v, folded, mask, spread, qkv,
     sq_own, sq_in, inv, bin_out, bin_in,
     load_sem, fold_send, fold_recv, seq_send, seq_recv,
@@ -119,6 +120,13 @@
     for q in range(seq_count):
         power_load(q).start()
 
+    indices = [
+        pltpu.make_async_copy(bin_hbm, bin_ref, load_sem.at[6]),
+        pltpu.make_async_copy(session_hbm, session_ref, load_sem.at[7]),
+    ]
+    for load in indices:
+        load.start()
+
     barrier = pltpu.get_barrier_semaphore()
 
     def greet(device):
@@ -157,8 +165,10 @@
         (seq + flip_x, 1 - y),
     )
 
+    nearest = (z, 1 + lax.rem(z, 2), lax.rem(2 + 3 * z, 5), 3 - 3 * lax.div(z, 2))
+
     def piece(line, t):
-        return lines[line][0], paired(z, t) * 2 + lines[line][1]
+        return lines[line][0], nearest[t] * 2 + lines[line][1]
 
     def fold_copy(at, sem, device):
         return pltpu.make_async_remote_copy(
@@ -172,7 +182,7 @@
 
     def along_z(t, act):
         at = piece(0, t)
-        here = paired(z, t)
+        here = nearest[t]
 
         @pl.when(jnp.logical_and(here <= z, z < 3))
         def _():
@@ -238,6 +248,10 @@
         if d:
             square_copy(d).start()
 
+    relay(0, 1)
+    for load in indices:
+        load.wait()
+
     rows = quarter * length
     device = wide * seq_count + seq
     session_row = session_ref[pl.ds(lax.div(device * quarter, 128), 1), :]
@@ -270,7 +284,7 @@
         jnp.broadcast_to((local_bin == b).astype(jnp.float32), (samples, CH)) for b in range(bins)
     ]
 
-    relay(0, 1)
+    relay(0, 2)
 
     total = sq_own[seq]
     for d in range(1, 4):
@@ -307,19 +321,18 @@
     def bin_copy(d):
         return seq_copy(2, bin_out.at[d], bin_in.at[d], d)
 
+    relay(0, 3)
+    relay(1, 0)
     bin_quarter(0, bin_in)
-    relay(0, 2)
+    relay(1, 1)
     for d in (2, 3, 1):
         inv_copy(d).wait_recv()
         bin_quarter(d, bin_out)
         bin_copy(d).start()
         if d == 2:
-            relay(0, 3)
-            relay(1, 0)
+            relay(1, 2)
         if d == 3:
-            relay(1, 1)
-    relay(1, 2)
-    relay(1, 3)
+            relay(1, 3)
     for t in range(4):
         relay(2, t)
     for t in range(4):
@@ -412,16 +425,18 @@
     columns = qkv_weight.shape[1] // seq_count
     rows = quarter * bins * seq_count
     width = readin_weight.shape[2]
-    hbm = pl.BlockSpec(memory_space=pl.ANY)
+    hbm = pl.BlockSpec(memory_space=pltpu.HBM)
     vmem = pl.BlockSpec(memory_space=pltpu.VMEM)
     bf16, f32 = jnp.bfloat16, jnp.float32
     dma = pltpu.SemaphoreType.DMA
     return pl.pallas_call(
         kernel,
         out_shape=jax.ShapeDtypeStruct((quarter, bins * seq_count, HEADS * HD), bf16),
-        in_specs=[hbm, vmem, vmem, hbm, hbm],
+        in_specs=[hbm] * 5,
         out_specs=vmem,
         scratch_shapes=[
+            pltpu.VMEM((1, samples), jnp.int32),
+            pltpu.VMEM((session.shape[0] // 128, 128), jnp.int32),
             pltpu.VMEM((samples, channels), bf16),
             pltpu.VMEM((CH, width), bf16),
             pltpu.VMEM((width, columns), bf16),
@@ -434,14 +449,14 @@
             pltpu.VMEM((seq_count, quarter, CH), f32),
             pltpu.VMEM((seq_count, bins * quarter, CH), bf16),
             pltpu.VMEM((seq_count, bins * quarter, CH), bf16),
-            dma((6,)),
+            dma((8,)),
             dma((36,)),
             dma((seq_count, sessions)),
             dma((3, seq_count)),
             dma((3, seq_count)),
         ],
         compiler_params=pltpu.CompilerParams(
-            collective_id=0, has_side_effects=True, vmem_limit_bytes=40 * 2**20
+            collective_id=0, has_side_effects=True, vmem_limit_bytes=56 * 2**20
         ),
     )(power, bin_index.reshape(1, samples), session.reshape(-1, 128), readin_weight, qkv_weight)
 

time: 44.3 us -> 36.3 us (0.82)
  the two profiles are of different devices: /device:TPU:0 before, /device:TPU:1 now
where the time goes in v3:
time: 36.3 us; the launch traced here: 36.1 us
  Pallas kernels  33.8 us (93%)
  local copies, waits for them, and re-layouts  2.26 us (6%)
    pallas_call x1, Pallas kernels, fused(): pl.pallas_call(kernel, out_shape=jax.ShapeDtypeStruct((quarter, bins * se...  33.8 us
    unnamed x1, local copies, waits for them, and re-layouts  2.26 us

profile of v3, /device:TPU:1, one launch (start us, length us, event | category | flops | bytes accessed | tf_op | source)
XLA Modules:
  0.0 36.1 jit_solution(16004953695326144876)
XLA Ops:
  0.0 33.8 %shard_map.55 = bf16[64,8,1024]{2,1,0:T(8,128)(2,1)} custom-call(bf16[40,32768]{1,0:T(8,128)(2,1)} %power_hbm.1, s32[1,40]{1,0:T(1,128)} %bitcast.3, s32[16,128]{1,0:T(8,128)} %bitcast.2, bf16[1,128,2048]{2,1,0:T(8,128)(2,1)} %readin_hbm.1, bf16[2048,1536]{1,0:T(8,128)(2,1)} %weight_hbm.1), custom_call_target="tpu_custom_call" | custom-call | tf_op jit(solution)/shard_map/pallas_call | solution.py:432
  33.8 2.3 %copy.7 = bf16[64,8,1024]{2,1,0:T(8,128)(2,1)} copy(bf16[64,8,1024]{2,1,0:T(8,128)(2,1)} %shard_map.55) | data formatting | bytes 2097152

commit v4 on v3

--- a/solution.py
+++ b/solution.py
@@ -81,9 +81,9 @@
 
 
 def kernel(
-    power_hbm, bin_hbm, session_hbm, readin_hbm, weight_hbm, out_ref,
+    power_hbm, bin_hbm, session_hbm, readin_hbm, weight_hbm, qkv_ref,
     bin_ref, session_ref,
-    power_v, readin_v, weight_v, folded, mask, spread, qkv,
+    power_v, readin_v, weight_v, folded, mask, spread,
     sq_own, sq_in, inv, bin_out, bin_in,
     load_sem, fold_send, fold_recv, seq_send, seq_recv,
 ):
@@ -360,51 +360,21 @@
         at = slice(n * block, (n + 1) * block)
         spread[at, :] = mask[at, :] * jnp.concatenate([turned] * sessions, axis=1)
 
+    def project(owner):
+        at = pl.ds(pl.multiple_of(owner * columns, 128), columns)
+        weights = folded[owner].reshape(sessions * CH, columns)
+        qkv_ref[:, at] = jnp.dot(
+            spread[...], weights, preferred_element_type=jnp.float32
+        ).astype(jnp.bfloat16)
+
+    project(seq)
+    project(seq + flip_x)
     for line in range(4):
         for t in range(4):
             at = piece(line, t)
             fold_copy((at[0] + 1 - 2 * core, at[1]), 0, other_core).wait_recv()
-
-    for n in range(seq_count):
-        weights = folded[n].reshape(sessions * CH, columns)
-        qkv[:, n * columns : (n + 1) * columns] = jnp.dot(
-            spread[...], weights, preferred_element_type=jnp.float32
-        ).astype(jnp.bfloat16)
-
-    group = HEADS // KVH
-    same = lax.div(lax.broadcasted_iota(jnp.int32, (group * block, block), 0), length)
-    same = lax.rem(same, 16) == lax.div(
-        lax.broadcasted_iota(jnp.int32, (group * block, block), 1), length
-    )
-
-    @pl.loop(0, quarter // 16)
-    def _(n):
-        at = pl.ds(pl.multiple_of(n * block, block), block)
-
-        def normed(h, scale):
-            values = qkv[at, h * HD : (h + 1) * HD].astype(jnp.float32)
-            mean = jnp.mean(values * values, axis=-1, keepdims=True)
-            return (values * (lax.rsqrt(mean + 1e-06) * scale)).astype(jnp.bfloat16)
-
-        for g in range(KVH):
-            keys = normed(HEADS + g, 1.0)
-            heads = range(g * group, (g + 1) * group)
-            queries = jnp.concatenate([normed(h, HD**-0.5) for h in heads], axis=0)
-            scores = lax.dot_general(
-                queries, keys, (((1,), (1,)), ((), ())), preferred_element_type=jnp.float32
-            )
-            exponent = jnp.where(same, jnp.exp(scores), 0.0)
-            weights = exponent * (1.0 / jnp.sum(exponent, axis=-1, keepdims=True))
-            mixed = jnp.dot(
-                weights.astype(jnp.bfloat16),
-                qkv[at, (HEADS + KVH + g) * HD : (HEADS + KVH + g + 1) * HD],
-                preferred_element_type=jnp.float32,
-            )
-            for i, h in enumerate(heads):
-                own_rows = mixed[i * block : (i + 1) * block].reshape(16, length, HD)
-                out_ref[pl.ds(n * 16, 16), :, h * HD : (h + 1) * HD] = own_rows.astype(
-                    jnp.bfloat16
-                )
+    project(seq + 1 - 2 * core)
+    project(seq + flip_x + 1 - 2 * core)
 
     for d in range(1, 4):
         square_copy(d).wait_send()
@@ -415,6 +385,41 @@
             if line == 0:
                 along_z(t, wait_send)
             onward(line, t, wait_send)
+
+
+def attention(qkv_ref, out_ref):
+    patches, length, _ = out_ref.shape
+    block = patches * length
+    group = HEADS // KVH
+    same = lax.div(lax.broadcasted_iota(jnp.int32, (group * block, block), 0), length)
+    same = lax.rem(same, patches) == lax.div(
+        lax.broadcasted_iota(jnp.int32, (group * block, block), 1), length
+    )
+
+    def normed(h, scale):
+        values = qkv_ref[:, h * HD : (h + 1) * HD].astype(jnp.float32)
+        mean = jnp.mean(values * values, axis=-1, keepdims=True)
+        return (values * (lax.rsqrt(mean + 1e-06) * scale)).astype(jnp.bfloat16)
+
+    for g in range(KVH):
+        keys = normed(HEADS + g, 1.0)
+        heads = range(g * group, (g + 1) * group)
+        queries = jnp.concatenate([normed(h, HD**-0.5) for h in heads], axis=0)
+        scores = lax.dot_general(
+            queries, keys, (((1,), (1,)), ((), ())), preferred_element_type=jnp.float32
+        )
+        exponent = jnp.where(same, jnp.exp(scores), 0.0)
+        weights = exponent * (1.0 / jnp.sum(exponent, axis=-1, keepdims=True))
+        mixed = jnp.dot(
+            weights.astype(jnp.bfloat16),
+            qkv_ref[:, (HEADS + KVH + g) * HD : (HEADS + KVH + g + 1) * HD],
+            preferred_element_type=jnp.float32,
+        )
+        for i, h in enumerate(heads):
+            own_rows = mixed[i * block : (i + 1) * block].reshape(patches, length, HD)
+            out_ref[:, :, h * HD : (h + 1) * HD] = own_rows.astype(
+                jnp.bfloat16
+            )
 
 
 def fused(power, bin_index, session, readin_weight, qkv_weight):
@@ -429,9 +434,9 @@
     vmem = pl.BlockSpec(memory_space=pltpu.VMEM)
     bf16, f32 = jnp.bfloat16, jnp.float32
     dma = pltpu.SemaphoreType.DMA
-    return pl.pallas_call(
+    qkv = pl.pallas_call(
         kernel,
-        out_shape=jax.ShapeDtypeStruct((quarter, bins * seq_count, HEADS * HD), bf16),
+        out_shape=jax.ShapeDtypeStruct((rows, qkv_weight.shape[1]), bf16),
         in_specs=[hbm] * 5,
         out_specs=vmem,
         scratch_shapes=[
@@ -443,7 +448,6 @@
             pltpu.VMEM((seq_count, sessions, CH, columns), bf16),
             pltpu.VMEM((rows, sessions * CH), bf16),
             pltpu.VMEM((rows, sessions * CH), bf16),
-            pltpu.VMEM((rows, qkv_weight.shape[1]), bf16),
             pltpu.VMEM((seq_count, quarter, CH), f32),
             pltpu.VMEM((seq_count, quarter, CH), f32),
             pltpu.VMEM((seq_count, quarter, CH), f32),
@@ -459,6 +463,14 @@
             collective_id=0, has_side_effects=True, vmem_limit_bytes=56 * 2**20
         ),
     )(power, bin_index.reshape(1, samples), session.reshape(-1, 128), readin_weight, qkv_weight)
+    length = bins * seq_count
+    return pl.pallas_call(
+        attention,
+        grid=(quarter // 16,),
+        out_shape=jax.ShapeDtypeStruct((quarter, length, HEADS * HD), bf16),
+        in_specs=[pl.BlockSpec((16 * length, qkv.shape[1]), lambda n: (n, 0))],
+        out_specs=pl.BlockSpec((16, length, HEADS * HD), lambda n: (n, 0, 0)),
+    )(qkv)
 
 
 def solution(mesh):

time: 36.3 us -> 35.7 us (0.983)
  the two profiles are of different devices: /device:TPU:1 before, /device:TPU:0 now
where the time goes in v4:
time: 35.7 us; the launch traced here: 35.6 us
  Pallas kernels  35.6 us (100%)
    pallas_call x1, Pallas kernels, fused(): pl.pallas_call(kernel, out_shape=jax.ShapeDtypeStruct((rows, qkv_weight.s...  30.3 us
    pallas_call x1, Pallas kernels, fused(): pl.pallas_call(attention, grid=(quarter // 16,), out_shape=jax.ShapeDtype...  5.25 us

profile of v4, /device:TPU:0, one launch (start us, length us, event | category | flops | bytes accessed | tf_op | source)
XLA Modules:
  0.0 35.6 jit_solution(16779610697314234027)
XLA Ops:
  0.0 30.3 %shard_map.55.qkv_ref = bf16[512,1536]{1,0:T(8,128)(2,1)} custom-call(bf16[40,32768]{1,0:T(8,128)(2,1)} %power_hbm.1, s32[1,40]{1,0:T(1,128)} %bitcast.3, s32[16,128]{1,0:T(8,128)} %bitcast.2, bf16[1,128,2048]{2,1,0:T(8,128)(2,1)} %readin_hbm.1, bf16[2048,1536]{1,0:T(8,128)(2,1)} %weight_hbm.1), custom_call_target="tpu_custom_call" | custom-call | tf_op jit(solution)/shard_map/pallas_call | solution.py:437
  30.3 5.3 %shard_map.56 = bf16[64,8,1024]{2,1,0:T(8,128)(2,1)} custom-call(bf16[512,1536]{1,0:T(8,128)(2,1)} %shard_map.55.qkv_ref), custom_call_target="tpu_custom_call" | custom-call | tf_op jit(solution)/shard_map/pallas_call | solution.py:467

commit v5 on v4

--- a/solution.py
+++ b/solution.py
@@ -396,10 +396,14 @@
         lax.broadcasted_iota(jnp.int32, (group * block, block), 1), length
     )
 
+    ones = jnp.ones((HD, HD), jnp.bfloat16)
+
     def normed(h, scale):
         values = qkv_ref[:, h * HD : (h + 1) * HD].astype(jnp.float32)
-        mean = jnp.mean(values * values, axis=-1, keepdims=True)
-        return (values * (lax.rsqrt(mean + 1e-06) * scale)).astype(jnp.bfloat16)
+        total = jnp.dot(
+            (values * values).astype(jnp.bfloat16), ones, preferred_element_type=jnp.float32
+        )
+        return (values * (lax.rsqrt(total / HD + 1e-06) * scale)).astype(jnp.bfloat16)
 
     for g in range(KVH):
         keys = normed(HEADS + g, 1.0)
@@ -409,12 +413,13 @@
             queries, keys, (((1,), (1,)), ((), ())), preferred_element_type=jnp.float32
         )
         exponent = jnp.where(same, jnp.exp(scores), 0.0)
-        weights = exponent * (1.0 / jnp.sum(exponent, axis=-1, keepdims=True))
-        mixed = jnp.dot(
-            weights.astype(jnp.bfloat16),
-            qkv_ref[:, (HEADS + KVH + g) * HD : (HEADS + KVH + g + 1) * HD],
+        values = qkv_ref[:, (HEADS + KVH + g) * HD : (HEADS + KVH + g + 1) * HD]
+        summed = jnp.dot(
+            exponent.astype(jnp.bfloat16),
+            jnp.concatenate([values, ones[:block]], axis=1),
             preferred_element_type=jnp.float32,
         )
+        mixed = summed[:, :HD] * (1.0 / summed[:, HD:])
         for i, h in enumerate(heads):
             own_rows = mixed[i * block : (i + 1) * block].reshape(patches, length, HD)
             out_ref[:, :, h * HD : (h + 1) * HD] = own_rows.astype(

time: 35.7 us -> 36.2 us (1.014)
  Pallas kernels: 35.6 us -> 36 us
    pallas_call x1, Pallas kernels: 5.25 us -> 5.7 us  [fused(): pl.pallas_call(attention, grid=(quarter // 16,), out_shape=jax.ShapeDtype...]
where the time goes in v5:
time: 36.2 us; the launch traced here: 36 us
  Pallas kernels  36 us (99%)
    pallas_call x1, Pallas kernels, fused(): pl.pallas_call(kernel, out_shape=jax.ShapeDtypeStruct((rows, qkv_weight.s...  30.3 us
    pallas_call x1, Pallas kernels, fused(): pl.pallas_call(attention, grid=(quarter // 16,), out_shape=jax.ShapeDtype...  5.7 us

profile of v5, /device:TPU:0, one launch (start us, length us, event | category | flops | bytes accessed | tf_op | source)
XLA Modules:
  0.0 36.0 jit_solution(3470430583707167571)
XLA Ops:
  0.0 30.3 %shard_map.55.qkv_ref = bf16[512,1536]{1,0:T(8,128)(2,1)} custom-call(bf16[40,32768]{1,0:T(8,128)(2,1)} %power_hbm.1, s32[1,40]{1,0:T(1,128)} %bitcast.3, s32[16,128]{1,0:T(8,128)} %bitcast.2, bf16[1,128,2048]{2,1,0:T(8,128)(2,1)} %readin_hbm.1, bf16[2048,1536]{1,0:T(8,128)(2,1)} %weight_hbm.1), custom_call_target="tpu_custom_call" | custom-call | tf_op jit(solution)/shard_map/pallas_call | solution.py:442
  30.3 5.7 %shard_map.56 = bf16[64,8,1024]{2,1,0:T(8,128)(2,1)} custom-call(bf16[512,1536]{1,0:T(8,128)(2,1)} %shard_map.55.qkv_ref), custom_call_target="tpu_custom_call" | custom-call | tf_op jit(solution)/shard_map/pallas_call | solution.py:472
